TPU v7x, 32 devices: a whole 2x2x4 slice. The times are simulated.
32 devices in a mesh: groups: 2 (over y), seq: 8 (over z, core), panel: 2 (over x).
Axes of the slice: x: 2, y: 2, z: 4, core: 2. Of those that a mesh axis runs over, the one named last changes fastest.
Arguments:
- queries: bfloat16 [4096, 3072], P(('groups', 'seq'), 'panel'), parts along dimension 0, may hold values from -120 to 120
- key_rows: bfloat16 [4096, 3072], P(('groups', 'seq'), 'panel'), parts along dimension 0, may hold values from -6 to 6
- value_rows: bfloat16 [4096, 3072], P(('groups', 'seq'), 'panel'), parts along dimension 0, may hold values from -6 to 6
- block_lists: int32 [24, 16, 8], P('panel'), may hold values from 0 to 15, as said below
- block_counts: int32 [24, 16], P('panel'), may hold values from 4 to 8, as said below
Outputs:
- attended: bfloat16 [4096, 3072], P(('groups', 'seq', 'panel')), parts along dimension 0
There are 2 independent parts, one for each index of `groups`. A program takes and returns all parts, laid end to end along the dimension named above; an argument that names none is the same for every part. Nothing has to cross between parts.
Inputs may be any that keep to these rules, and one draw needn't show every extreme that they name: `block_lists`: entry 0 of each list is the tile's own block index; the entries of one list are distinct; for each head, the lists of the 2 tiles held by one index of seq name together at most 1 distinct blocks among the 2 blocks of any other index of seq, and exactly 1 of some other index. `block_counts`: some list has all 8 entries live.
All inputs are finite; a program needn't handle non-finite values.
Results may differ from a plain program's by a relative error of at most 0.008.
Values may be sent and summed in bfloat16 or wider, within the bound.
A program may use at most 128 MiB of HBM per device.

v0:
```python
import jax
import jax.numpy as jnp
from jax import lax
from jax.sharding import PartitionSpec as P

HEAD_DIM = 128
BLOCK = 128


def shards(queries, key_rows, value_rows, block_lists, block_counts):
    local_rows = queries.shape[0]
    heads_here = queries.shape[1] // HEAD_DIM
    tiles_here = local_rows // BLOCK
    listed_len = block_lists.shape[2]
    scale = HEAD_DIM ** (-0.5)
    position = lax.axis_index("seq")
    my_lists = lax.dynamic_slice_in_dim(block_lists, position * tiles_here, tiles_here, 1)
    my_counts = lax.dynamic_slice_in_dim(block_counts, position * tiles_here, tiles_here, 1)
    slot_live = jnp.arange(listed_len, dtype=jnp.int32)[None, None, :] < my_counts[:, :, None]
    query_heads = queries.reshape(local_rows, heads_here, HEAD_DIM).transpose(1, 0, 2)
    start_top = jnp.full((heads_here, local_rows), -1e30, jnp.float32)
    start_total = jnp.zeros((heads_here, local_rows), jnp.float32)
    start_mixed = jnp.zeros((heads_here, local_rows, HEAD_DIM), jnp.float32)
    key_piece = lax.all_gather(key_rows, "seq", axis=0, tiled=True)
    value_piece = lax.all_gather(value_rows, "seq", axis=0, tiled=True)
    piece_rows = key_piece.shape[0]
    piece_blocks = piece_rows // BLOCK
    piece_ids = jnp.arange(piece_blocks, dtype=jnp.int32)
    hits = (my_lists[:, :, :, None] == piece_ids[None, None, None, :]) & slot_live[:, :, :, None]
    keep = jnp.any(hits, axis=2)
    key_heads = key_piece.reshape(piece_rows, heads_here, HEAD_DIM).transpose(1, 0, 2)
    value_heads = value_piece.reshape(piece_rows, heads_here, HEAD_DIM).transpose(1, 0, 2)

    def one_head(items):
        query_head, key_head, value_head, keep_head, old_top, old_total, old_mixed = items
        mask = jnp.repeat(jnp.repeat(keep_head, BLOCK, axis=0), BLOCK, axis=1)
        scores = (
            lax.dot_general(
                query_head, key_head, (((1,), (1,)), ((), ())), preferred_element_type=jnp.float32
            )
            * scale
        )
        masked = jnp.where(mask, scores, -1e30)
        new_top = jnp.maximum(old_top, jnp.max(masked, axis=1))
        weights = jnp.where(mask, jnp.exp(masked - new_top[:, None]), 0.0)
        factor = jnp.exp(old_top - new_top)
        new_total = old_total * factor + jnp.sum(weights, axis=1)
        rounded = weights.astype(jnp.bfloat16)
        new_mixed = old_mixed * factor[:, None] + jnp.dot(
            rounded, value_head, preferred_element_type=jnp.float32
        )
        return (new_top, new_total, new_mixed)

    final_top, final_total, final_mixed = lax.map(
        one_head, (query_heads, key_heads, value_heads, keep, start_top, start_total, start_mixed)
    )
    results = (final_mixed / final_total[:, :, None]).astype(jnp.bfloat16)
    joined = results.transpose(1, 0, 2).reshape(local_rows, heads_here * HEAD_DIM)
    return lax.all_to_all(joined, "panel", split_axis=0, concat_axis=1, tiled=True)


def solution(mesh):
    return jax.shard_map(
        shards,
        mesh=mesh,
        in_specs=(
            P(("groups", "seq"), "panel"),
            P(("groups", "seq"), "panel"),
            P(("groups", "seq"), "panel"),
            P("panel", None, None),
            P("panel", None),
        ),
        out_specs=P(("groups", "seq", "panel"), None),
        check_vma=False,
    )
```

profile of v0, /device:TPU:0, one launch (start us, length us, event | category | flops | bytes accessed | tf_op | source)
XLA Modules:
  0.0 240.2 jit_solution(3011953316735453202)
XLA Ops:
  6.5 2.4 %copy.37 = bf16[256,1536]{0,1:T(8,128)(2,1)} copy(bf16[256,1536]{1,0:T(8,128)(2,1)} %param.8) | data formatting | bytes 1572864 | tf_op args[1]
  9.0 1.2 copy.38
  10.3 0.1 constant_dynamic-slice_fusion.1
  10.4 0.1 copy.35
  10.5 0.3 copy.36
  10.9 0.1 iota_compare_fusion.1
  11.0 0.1 fusion.19
  11.1 65.9 %all-gather.3.cloned.1.call-done = bf16[2048,1536]{0,1:T(8,128)(2,1)} async-done(((bf16[256,1536]{0,1:T(8,128)(2,1)}), bf16[2048,1536]{0,1:T(8,128)(2,1)}) %all-gather.3.cloned.1.call-update) | async-done | bytes 6291472 | tf_op jit(solution)/shard_map/all_gather | solution.py:24
  77.1 65.0 %all-gather.5.cloned.1.call-done = bf16[2048,1536]{0,1:T(8,128)(2,1)} async-done(((bf16[256,1536]{0,1:T(8,128)(2,1)}), bf16[2048,1536]{0,1:T(8,128)(2,1)}) %all-gather.5.cloned.1.call-update) | async-done | bytes 6291472 | tf_op jit(solution)/shard_map/all_gather | solution.py:25
  142.0 73.7 %while.12 = (s32[]{:T(128)}, f32[12,256]{1,0:T(8,128)S(1)}, f32[12,256,128]{2,1,0:T(8,128)}, pred[12,2,16]{2,1,0:T(4,128)(4,1)S(1)}, bf16[12,256,128]{1,2,0:T(8,...) while((s32[]{:T(128)}, f32[12,256]{1,0:T(8,128)S(1)}, ...), condition=%wide.region_4.5_spmd, body=%wide.region_1.4_spmd.sunk | while | flops 273187584 | bytes 9657549 | solution.py:54
  142.1 1.3 broadcast_in_dim.39
  143.3 1.8 fusion.28
  145.1 0.6 fusion.29
  145.8 2.4 fusion.30
  148.2 1.3 broadcast_in_dim.39
  149.5 1.8 fusion.28
  151.2 0.6 fusion.29
  152.0 2.4 fusion.30
  154.3 1.3 broadcast_in_dim.39
  155.6 1.8 fusion.28
  157.4 0.6 fusion.29
  158.1 2.4 fusion.30
  160.5 1.3 broadcast_in_dim.39
  161.8 1.8 fusion.28
  163.5 0.6 fusion.29
  164.2 2.4 fusion.30
  166.6 1.3 broadcast_in_dim.39
  167.9 1.8 fusion.28
  169.7 0.6 fusion.29
  170.4 2.4 fusion.30
  172.8 1.3 broadcast_in_dim.39
  174.1 1.8 fusion.28
  175.8 0.6 fusion.29
  176.5 2.4 fusion.30
  178.9 1.3 broadcast_in_dim.39
  180.2 1.8 fusion.28
  182.0 0.6 fusion.29
  182.7 2.4 fusion.30
  185.1 1.3 broadcast_in_dim.39
  186.4 1.8 fusion.28
  188.1 0.6 fusion.29
  188.8 2.4 fusion.30
  191.2 1.3 broadcast_in_dim.39
  192.5 1.8 fusion.28
  194.3 0.6 fusion.29
  195.0 2.4 fusion.30
  197.4 1.3 broadcast_in_dim.39
  198.7 1.8 fusion.28
  200.4 0.6 fusion.29
  201.1 2.4 fusion.30
  203.5 1.3 broadcast_in_dim.39
  204.8 1.8 fusion.28
  206.6 0.6 fusion.29
  207.3 2.4 fusion.30
  209.6 1.3 broadcast_in_dim.39
  210.9 1.8 fusion.28
  212.7 0.6 fusion.29
  213.4 2.4 fusion.30
  215.8 1.9 fusion.17
  217.7 0.3 copy.42
  217.9 0.2 all_to_all.14
  218.1 0.1 copy.43
  218.2 13.9 %all_to_all.19 = bf16[2,128,1536]{1,2,0:T(8,128)(2,1)S(1)} all-to-all(bf16[2,128,1536]{1,2,0:T(8,128)(2,1)S(1)} %copy.43), channel_id=1, replica_groups=mesh['groups'=2,'seq'=8,'panel'=2] {'panel'}, dimensions={0} | all-to-all | bytes 1572864 | tf_op jit(solution)/shard_map/all_to_all | solution.py:59
  232.2 1.2 copy.44
  (75 shorter events, 1.1 us)
Async XLA Ops:
  6.5 3.8 %copy-start = (s32[12,16,8]{1,2,0:T(8,128)S(1)}, s32[12,16,8]{1,2,0:T(8,128)}, u32[]{:S(2)}) copy-start(s32[12,16,8]{1,2,0:T(8,128)} %param.10) | copy-start | bytes 18436
  6.5 2.5 %copy-start.1 = (bf16[256,1536]{1,0:T(8,128)(2,1)S(1)}, bf16[256,1536]{1,0:T(8,128)(2,1)}, u32[]{:S(2)}) copy-start(bf16[256,1536]{1,0:T(8,128)(2,1)} %param.9) | copy-start | bytes 2359300
  6.5 4.0 %copy-start.2 = (bf16[256,1536]{1,0:T(8,128)(2,1)S(1)}, bf16[256,1536]{1,0:T(8,128)(2,1)}, u32[]{:S(2)}) copy-start(bf16[256,1536]{1,0:T(8,128)(2,1)} %param.7) | copy-start | bytes 2359300
  6.5 70.5 %all-gather.3.cloned.1.call-start = ((), (), s32[]{:S(2)}) async-start(), calls=%async_computation.1 | async-start | bytes 7077888 | tf_op jit(solution)/shard_map/all_gather | solution.py:24
  9.0 1.8 copy-start.3
  9.0 133.0 %all-gather.5.cloned.1.call-start = ((), (), s32[]{:S(2)}) async-start(), calls=%async_computation.2 | async-start | bytes 7077888 | tf_op jit(solution)/shard_map/all_gather | solution.py:25
Sparse Core Ops, SparseCore 0:
  9.1 67.9 all-gather.2
  78.6 63.3 all-gather.4
where the time goes:
time: 242 us; the launch traced here: 240 us
  waiting for transfers between devices  131 us (54%)
  matrix products  49.4 us (20%)
  local copies, waits for them, and re-layouts  22.1 us (9%)
  blocking collectives  13.9 us (6%)
  between operations  13.5 us (6%)
  other arithmetic  10.1 us (4%)
    all_gather x1, waiting for transfers between devices, shards(): key_piece = lax.all_gather(key_rows, 'seq', axis=0, tiled=True)  65.9 us
    all_gather x1, waiting for transfers between devices, shards(): value_piece = lax.all_gather(value_rows, 'seq', axis=0, tiled=True)  65 us
    dot_general x12, matrix products, one_head(): jnp.dot(rounded, value_head, preferred_element_type=jnp.float32)  28.3 us
    dot_general x12, matrix products, one_head(): lax.dot_general(query_head, key_head, (((1,), (1,)), ((), ())), preferred...  21.1 us
    broadcast_in_dim x24, local copies, waits for them, and re-layouts, one_head(): mask = jnp.repeat(jnp.repeat(keep_head, BLOCK, axis=0), BLOCK, axis=1)  15.6 us
    all_to_all x1, blocking collectives, shards(): lax.all_to_all(joined, 'panel', split_axis=0, concat_axis=1, tiled=True)  13.9 us
    reduce_sum x12, other arithmetic, one_head(): new_total = old_total * factor + jnp.sum(weights, axis=1)  7.78 us
  transfers between devices with their start and end apart: 2, of which 2 were waited for; matrix products, arithmetic and copies ran while one was open for 1% of the time, Pallas kernels for 0%

commit v1 on v0

v1 whole, which is shorter than its diff:
```python
import functools

import jax
import jax.numpy as jnp
from jax import lax
from jax.experimental import pallas as pl
from jax.experimental.pallas import tpu as pltpu
from jax.sharding import PartitionSpec as P

HEAD_DIM = 128
BLOCK = 128
CORES = 2
MESH = pl.DeviceIdType.MESH


def gathered(queries, key_rows, value_rows, block_lists, block_counts):
    local_rows = queries.shape[0]
    heads_here = queries.shape[1] // HEAD_DIM
    tiles_here = local_rows // BLOCK
    listed_len = block_lists.shape[2]
    scale = HEAD_DIM ** (-0.5)
    position = lax.axis_index("seq")
    my_lists = lax.dynamic_slice_in_dim(block_lists, position * tiles_here, tiles_here, 1)
    my_counts = lax.dynamic_slice_in_dim(block_counts, position * tiles_here, tiles_here, 1)
    slot_live = jnp.arange(listed_len, dtype=jnp.int32)[None, None, :] < my_counts[:, :, None]
    query_heads = queries.reshape(local_rows, heads_here, HEAD_DIM).transpose(1, 0, 2)
    key_piece = lax.all_gather(key_rows, "seq", axis=0, tiled=True)
    value_piece = lax.all_gather(value_rows, "seq", axis=0, tiled=True)
    piece_rows = key_piece.shape[0]
    piece_ids = jnp.arange(piece_rows // BLOCK, dtype=jnp.int32)
    hits = (my_lists[:, :, :, None] == piece_ids[None, None, None, :]) & slot_live[:, :, :, None]
    keep = jnp.any(hits, axis=2)
    key_heads = key_piece.reshape(piece_rows, heads_here, HEAD_DIM).transpose(1, 0, 2)
    value_heads = value_piece.reshape(piece_rows, heads_here, HEAD_DIM).transpose(1, 0, 2)

    def one_head(items):
        query_head, key_head, value_head, keep_head = items
        mask = jnp.repeat(jnp.repeat(keep_head, BLOCK, axis=0), BLOCK, axis=1)
        scores = (
            lax.dot_general(
                query_head, key_head, (((1,), (1,)), ((), ())), preferred_element_type=jnp.float32
            )
            * scale
        )
        masked = jnp.where(mask, scores, -1e30)
        top = jnp.max(masked, axis=1, keepdims=True)
        weights = jnp.where(mask, jnp.exp(masked - top), 0.0)
        total = jnp.sum(weights, axis=1, keepdims=True)
        mixed = jnp.dot(weights.astype(jnp.bfloat16), value_head, preferred_element_type=jnp.float32)
        return (mixed / total).astype(jnp.bfloat16)

    results = lax.map(one_head, (query_heads, key_heads, value_heads, keep))
    joined = results.transpose(1, 0, 2).reshape(local_rows, heads_here * HEAD_DIM)
    return lax.all_to_all(joined, "panel", split_axis=0, concat_axis=1, tiled=True)


def spread_kernel(
    n, panels, heads, trio,
    lists, counts, q, k, v, out,
    qf, kf, vf, qs, ks, vs, of, os,
    fsend, frecv, qsend, qrecv, csend, crecv, wsend, osend, orecv,
):
    me = lax.axis_index("seq")
    pan = lax.axis_index("panel")
    chip, core = me // CORES, me % CORES
    chips = n // CORES
    sibling = chip * CORES + 1 - core
    held = q.shape[0]
    listed = lists.shape[2]
    tiles = n * panels
    scale = HEAD_DIM ** (-0.5)
    flat = me * panels + pan

    def columns(head):
        return pl.ds(pl.multiple_of(head * HEAD_DIM, HEAD_DIM), HEAD_DIM)

    def span(at, size):
        return pl.ds(pl.multiple_of(at * size, size), size)

    def whole_head(device):
        return (device // CORES) * trio + device % CORES

    def shared_head(device):
        return (device // CORES) * trio + CORES

    def full_copy(kind, step, device):
        src, dst = ((k, kf), (q, qf), (v, vf))[kind]
        return pltpu.make_async_remote_copy(
            src_ref=src.at[:, :, columns(whole_head(device))],
            dst_ref=dst.at[span(me, held)],
            send_sem=fsend.at[kind, step],
            recv_sem=frecv.at[kind, me],
            device_id={"seq": device},
            device_id_type=MESH,
        )

    def query_copy(step, device):
        return pltpu.make_async_remote_copy(
            src_ref=q.at[device % CORES, :, columns(shared_head(device))],
            dst_ref=qs.at[me],
            send_sem=qsend.at[step],
            recv_sem=qrecv.at[me],
            device_id={"seq": device},
            device_id_type=MESH,
        )

    def shared_copy(kind, step, device):
        src, dst = ((k, ks), (v, vs))[kind]
        return pltpu.make_async_remote_copy(
            src_ref=src.at[:, :, columns(shared_head(device))],
            dst_ref=dst.at[span(me, held)],
            send_sem=csend.at[kind, step],
            recv_sem=crecv.at[kind, me],
            device_id={"seq": device},
            device_id_type=MESH,
        )

    def forward_copy(kind, step, origin):
        buf = (ks, vs)[kind]
        return pltpu.make_async_remote_copy(
            src_ref=buf.at[span(origin, held)],
            dst_ref=buf.at[span(origin, held)],
            send_sem=wsend.at[kind, step],
            recv_sem=crecv.at[kind, origin],
            device_id={"seq": sibling},
            device_id_type=MESH,
        )

    def result_copy(buf, index, slot, head, tile):
        return pltpu.make_async_remote_copy(
            src_ref=buf.at[index],
            dst_ref=out.at[:, columns(pan * heads + head)],
            send_sem=osend.at[slot],
            recv_sem=orecv.at[pan * heads + head],
            device_id={"seq": tile // panels, "panel": tile % panels},
            device_id_type=MESH,
        )

    barrier = pltpu.get_barrier_semaphore()

    def greet(step, carry):
        other = (flat + step) % (n * panels)
        pl.semaphore_signal(
            barrier, inc=1,
            device_id={"seq": other // panels, "panel": other % panels},
            device_id_type=MESH,
        )
        return carry

    lax.fori_loop(1, n * panels, greet, 0)

    own = [
        pltpu.make_async_copy(src.at[:, :, columns(whole_head(me))], dst.at[span(me, held)], frecv.at[kind, me])
        for kind, (src, dst) in enumerate(((k, kf), (q, qf), (v, vf)))
    ]
    own.append(
        pltpu.make_async_copy(
            q.at[core, :, columns(shared_head(me))], qs.at[me], qrecv.at[me]
        )
    )
    own += [
        pltpu.make_async_copy(src.at[:, :, columns(shared_head(me))], dst.at[span(me, held)], crecv.at[kind, me])
        for kind, (src, dst) in enumerate(((k, ks), (v, vs)))
    ]
    for copy in own:
        copy.start()

    pl.semaphore_wait(barrier, n * panels - 1)

    def send_full(step, carry):
        device = (me + step) % n
        for kind in range(3):
            full_copy(kind, step, device).start()
        return carry

    lax.fori_loop(1, n, send_full, 0)

    def send_shared(step, carry):
        device = ((chip + step) % chips) * CORES + core
        for kind in range(2):
            shared_copy(kind, step, device).start()
        return carry

    lax.fori_loop(1, chips, send_shared, 0)
    for kind in range(2):
        shared_copy(kind, 0, sibling).start()

    def send_query(step, carry):
        query_copy(step, (me + step) % n).start()
        return carry

    lax.fori_loop(1, n, send_query, 0)

    def attend(query, head, tile, keys, values):
        blocks = [lists[head, tile, j] for j in range(listed)]
        live = counts[head, tile]
        scores = []
        for j in range(listed):
            dots = lax.dot_general(
                query, keys[blocks[j]], (((1,), (1,)), ((), ())), preferred_element_type=jnp.float32
            )
            scores.append(dots + jnp.minimum(live - 1 - j, 0).astype(jnp.float32) * 1e30)
        top = functools.reduce(jnp.maximum, scores)
        top = jnp.max(top, axis=1, keepdims=True)
        weights = [jnp.exp((s - top) * scale) for s in scores]
        total = jnp.sum(functools.reduce(jnp.add, weights), axis=1, keepdims=True)
        mixed = functools.reduce(
            jnp.add,
            [
                jnp.dot(w.astype(jnp.bfloat16), values[blocks[j]], preferred_element_type=jnp.float32)
                for j, w in enumerate(weights)
            ],
        )
        return (mixed / total).astype(jnp.bfloat16)

    def ship(buf, index, slot, head, tile):
        home = tile == flat

        @pl.when(home)
        def _():
            pltpu.make_async_copy(
                buf.at[index], out.at[:, columns(pan * heads + head)], orecv.at[pan * heads + head]
            ).start()

        @pl.when(jnp.logical_not(home))
        def _():
            result_copy(buf, index, slot, head, tile).start()

    def wait_full(src, carry):
        for kind, (ref, dst) in enumerate(((k, kf), (q, qf), (v, vf))):
            pltpu.make_async_copy(
                ref.at[:, :, columns(0)], dst.at[span(src, held)], frecv.at[kind, src]
            ).wait()
        return carry

    lax.fori_loop(0, n, wait_full, 0)

    def full_pair(step, carry):
        device = (me + step) % n
        mine = whole_head(me)
        for place in range(panels):
            tile = device * panels + place
            of[tile] = attend(qf[tile], mine, tile, kf, vf)
            ship(of, tile, tile, mine, tile)
        return carry

    lax.fori_loop(1, n + 1, full_pair, 0)

    def wait_shared(kind, origin):
        ref, dst = ((k, ks), (v, vs))[kind]
        pltpu.make_async_copy(
            ref.at[:, :, columns(0)], dst.at[span(origin, held)], crecv.at[kind, origin]
        ).wait()

    def forward(step, carry):
        origin = ((chip + step) % chips) * CORES + core
        for kind in range(2):
            wait_shared(kind, origin)
            forward_copy(kind, step, origin).start()
        return carry

    lax.fori_loop(1, chips, forward, 0)
    for kind in range(2):
        wait_shared(kind, me)

    def wait_query(src, carry):
        pltpu.make_async_copy(
            q.at[0, :, columns(0)], qs.at[src], qrecv.at[src]
        ).wait()
        return carry

    lax.fori_loop(0, n, wait_query, 0)

    def wait_other(step, carry):
        for kind in range(2):
            wait_shared(kind, step * CORES + 1 - core)
        return carry

    lax.fori_loop(0, chips, wait_other, 0)

    def half_pair(step, carry):
        mine = shared_head(me)
        for place in range(2):
            device = (me + 1 + step * 2 + place) % n
            tile = device * panels + core
            os[device] = attend(qs[device], mine, tile, ks, vs)
            ship(os, device, tiles + device, mine, tile)
        return carry

    lax.fori_loop(0, n // 2, half_pair, 0)

    def finish_sends(step, carry):
        device = (me + step) % n
        for kind in range(3):
            full_copy(kind, step, device).wait_send()
        query_copy(step, device).wait_send()
        return carry

    lax.fori_loop(1, n, finish_sends, 0)

    def finish_shared(step, carry):
        device = ((chip + step) % chips) * CORES + core
        for kind in range(2):
            shared_copy(kind, step, device).wait_send()
            forward_copy(kind, step, device).wait_send()
        return carry

    lax.fori_loop(1, chips, finish_shared, 0)
    for kind in range(2):
        shared_copy(kind, 0, sibling).wait_send()

    def finish_full_results(step, carry):
        tile = (flat + step) % tiles
        result_copy(of, tile, tile, whole_head(me), tile).wait_send()
        return carry

    lax.fori_loop(1, tiles, finish_full_results, 0)

    def finish_half_results(device, carry):
        tile = device * panels + core

        @pl.when(tile != flat)
        def _():
            result_copy(os, device, tiles + device, shared_head(me), tile).wait_send()

        return carry

    lax.fori_loop(0, n, finish_half_results, 0)

    def receive(head, carry):
        pltpu.make_async_copy(of.at[0], out.at[:, columns(head)], orecv.at[head]).wait()
        return carry

    lax.fori_loop(0, heads * panels, receive, 0)


def spread(n, panels, queries, key_rows, value_rows, block_lists, block_counts):
    rows, width = queries.shape
    heads = width // HEAD_DIM
    trio = CORES * heads // n
    tiles = n * panels
    kind = queries.dtype
    whole = pltpu.VMEM((tiles, BLOCK, HEAD_DIM), kind)
    dma = pltpu.SemaphoreType.DMA
    chips = n // CORES
    smem = pl.BlockSpec(memory_space=pltpu.SMEM)
    anywhere = pl.BlockSpec(memory_space=pl.ANY)
    return pl.pallas_call(
        functools.partial(spread_kernel, n, panels, heads, trio),
        out_shape=jax.ShapeDtypeStruct((BLOCK, width * panels), kind),
        in_specs=[smem, smem, anywhere, anywhere, anywhere],
        out_specs=anywhere,
        scratch_shapes=[
            whole, whole, whole,
            pltpu.VMEM((n, BLOCK, HEAD_DIM), kind), whole, whole,
            pltpu.VMEM((tiles, BLOCK, HEAD_DIM), kind),
            pltpu.VMEM((n, BLOCK, HEAD_DIM), kind),
            dma((3, n)), dma((3, n)),
            dma((n,)), dma((n,)),
            dma((2, chips)), dma((2, n)), dma((2, chips)),
            dma((tiles + n,)), dma((heads * panels,)),
        ],
        compiler_params=pltpu.CompilerParams(
            collective_id=0, has_side_effects=True, vmem_limit_bytes=48 * 1024 * 1024
        ),
        name="spread_heads",
    )(block_lists, block_counts, *(x.reshape(-1, BLOCK, width) for x in (queries, key_rows, value_rows)))


def solution(mesh):
    n, panels = mesh.shape["seq"], mesh.shape["panel"]

    def shards(queries, key_rows, value_rows, block_lists, block_counts):
        rows, width = queries.shape
        heads = width // HEAD_DIM
        fits = (
            n % CORES == 0
            and panels == CORES
            and rows == panels * BLOCK
            and CORES * heads == (CORES + 1) * n
        )
        if fits:
            return spread(n, panels, queries, key_rows, value_rows, block_lists, block_counts)
        return gathered(queries, key_rows, value_rows, block_lists, block_counts)

    return jax.shard_map(
        shards,
        mesh=mesh,
        in_specs=(
            P(("groups", "seq"), "panel"),
            P(("groups", "seq"), "panel"),
            P(("groups", "seq"), "panel"),
            P("panel", None, None),
            P("panel", None),
        ),
        out_specs=P(("groups", "seq", "panel"), None),
        check_vma=False,
    )
```

time: 242 us -> 84.3 us (0.35)
  waiting for transfers between devices: 131 us -> 0 us
  Pallas kernels: 0 us -> 78.6 us
  matrix products: 49.4 us -> 0 us
  local copies, waits for them, and re-layouts: 22.1 us -> 5.17 us
  blocking collectives: 13.9 us -> 0 us
  between operations: 13.5 us -> 0.04 us
  other arithmetic: 10.1 us -> 0 us
    all_gather x2 -> x0, waiting for transfers between devices: 131 us -> none  [the longest x1 65.9 us: shards(): key_piece = lax.all_gather(key_rows, 'seq', axis=0, tiled=True)]
    pallas_call x0 -> x1, Pallas kernels: none -> 78.6 us  [spread(): pl.pallas_call(functools.partial(spread_kernel, n, panels, heads, trio),...]
    dot_general x24 -> x0, matrix products: 49.4 us -> none  [the longest x12 28.3 us: one_head(): jnp.dot(rounded, value_head, preferred_element_type=jnp.float32)]
    broadcast_in_dim x24 -> x0, local copies, waits for them, and re-layouts: 15.6 us -> none  [one_head(): mask = jnp.repeat(jnp.repeat(keep_head, BLOCK, axis=0), BLOCK, axis=1)]
    all_to_all x1 -> x0, blocking collectives: 13.9 us -> none  [shards(): lax.all_to_all(joined, 'panel', split_axis=0, concat_axis=1, tiled=True)]
    reduce_sum x12 -> x0, other arithmetic: 7.78 us -> none  [one_head(): new_total = old_total * factor + jnp.sum(weights, axis=1)]
    unnamed x11 -> x10, local copies, waits for them, and re-layouts: 3.9 us -> 5.17 us
  transfers between devices with their start and end apart: 2 -> 0, of which waited for: 2 -> 0; matrix products, arithmetic and copies ran while one was open for 1% -> 0% of each run, Pallas kernels for 0% -> 0%
where the time goes in v1:
time: 84.3 us; the launch traced here: 83.9 us
  Pallas kernels  78.6 us (93%)
  local copies, waits for them, and re-layouts  5.17 us (6%)
    pallas_call x1, Pallas kernels, spread(): pl.pallas_call(functools.partial(spread_kernel, n, panels, heads, trio),...  78.6 us
    unnamed x10, local copies, waits for them, and re-layouts  5.17 us

profile of v1, /device:TPU:0, one launch (start us, length us, event | category | flops | bytes accessed | tf_op | source)
XLA Modules:
  0.0 83.9 jit_solution(16123831585314905984)
XLA Ops:
  0.0 0.0 copy-start.3
  0.0 0.9 %copy.6.lists = s32[12,16,8]{2,1,0:T(8,128)S(1)} copy(s32[12,16,8]{1,2,0:T(8,128)} %param.8) | data formatting | bytes 12288 | tf_op args[3]
  0.9 0.0 copy-done.3
  0.9 0.0 copy-start
  0.9 1.1 %copy-done = bf16[256,1536]{1,0:T(8,128)(2,1)S(1)} copy-done((bf16[256,1536]{1,0:T(8,128)(2,1)S(1)}, bf16[256,1536]{1,0:T(8,128)(2,1)}, u32[]{:S(2)}) %copy-start) | copy-done | bytes 786456
  2.0 0.0 copy-start.1
  2.0 1.1 %copy-done.1 = bf16[256,1536]{1,0:T(8,128)(2,1)S(1)} copy-done((bf16[256,1536]{1,0:T(8,128)(2,1)S(1)}, bf16[256,1536]{1,0:T(8,128)(2,1)}, u32[]{:S(2)}) %copy-start.1) | copy-done | bytes 786456
  3.2 0.0 copy-start.2
  3.2 1.1 %copy-done.2 = bf16[256,1536]{1,0:T(8,128)(2,1)S(1)} copy-done((bf16[256,1536]{1,0:T(8,128)(2,1)S(1)}, bf16[256,1536]{1,0:T(8,128)(2,1)}, u32[]{:S(2)}) %copy-start.2) | copy-done | bytes 786456
  4.3 78.6 %spread_heads.1 = bf16[128,3072]{1,0:T(8,128)(2,1)S(1)} custom-call(s32[12,16,8]{2,1,0:T(8,128)S(1)} %copy.6.lists, s32[12,16]{1,0:T(8,128)S(1)} %copy-done.3, bf16[2,128,1536]{2,1,0:T(8,128)(2,1)S(1)} %bitcast.3, bf16[2,128,1536]{2,1,0:T(8,128)(2,1)S(1)} %bitcast.4, bf16[2,128,1536]{2,1,0:T(8,128)(2,1)S(1)} %bitcast.5), custom_call_target="tpu_custom_call" | custom-call | tf_op jit(solution)/shard_map/spread_heads/pallas_call | solution.py:348
  83.0 0.9 %copy.8 = bf16[128,3072]{1,0:T(8,128)(2,1)} copy(bf16[128,3072]{1,0:T(8,128)(2,1)S(1)} %spread_heads.1) | data formatting | bytes 1572864
Async XLA Ops:
  0.0 0.9 %copy-start.3 = (s32[12,16]{1,0:T(8,128)S(1)}, s32[12,16]{1,0:T(8,128)}, u32[]{:S(2)}) copy-start(s32[12,16]{1,0:T(8,128)} %counts.1) | copy-start | bytes 2308
  0.9 1.1 %copy-start = (bf16[256,1536]{1,0:T(8,128)(2,1)S(1)}, bf16[256,1536]{1,0:T(8,128)(2,1)}, u32[]{:S(2)}) copy-start(bf16[256,1536]{1,0:T(8,128)(2,1)} %param.5) | copy-start | bytes 2359300
  2.0 1.1 %copy-start.1 = (bf16[256,1536]{1,0:T(8,128)(2,1)S(1)}, bf16[256,1536]{1,0:T(8,128)(2,1)}, u32[]{:S(2)}) copy-start(bf16[256,1536]{1,0:T(8,128)(2,1)} %param.6) | copy-start | bytes 2359300
  3.2 1.1 %copy-start.2 = (bf16[256,1536]{1,0:T(8,128)(2,1)S(1)}, bf16[256,1536]{1,0:T(8,128)(2,1)}, u32[]{:S(2)}) copy-start(bf16[256,1536]{1,0:T(8,128)(2,1)} %param.7) | copy-start | bytes 2359300

commit v2 on v1

--- a/solution.py
+++ b/solution.py
@@ -66,7 +66,7 @@
     chips = n // CORES
     sibling = chip * CORES + 1 - core
     held = q.shape[0]
-    listed = lists.shape[2]
+    listed = lists.shape[1]
     tiles = n * panels
     scale = HEAD_DIM ** (-0.5)
     flat = me * panels + pan
@@ -175,24 +175,189 @@
 
     lax.fori_loop(1, n, send_full, 0)
 
+    def sent_full(step):
+        for kind in range(3):
+            full_copy(kind, step, (me + step) % n).wait_send()
+        query_copy(step, (me + step) % n).start()
+
     def send_shared(step, carry):
+        sent_full(CORES * step - 1)
+        sent_full(CORES * step)
         device = ((chip + step) % chips) * CORES + core
         for kind in range(2):
             shared_copy(kind, step, device).start()
         return carry
 
     lax.fori_loop(1, chips, send_shared, 0)
+    sent_full(n - 1)
     for kind in range(2):
         shared_copy(kind, 0, sibling).start()
 
-    def send_query(step, carry):
+    def attend(query, head, tile, keys, values):
+        blocks = [lists[head, j, tile] for j in range(listed)]
+        live = counts[head, tile]
+        key_part = jnp.concatenate([keys[b] for b in blocks], axis=0)
+        dots = lax.dot_general(
+            query, key_part, (((1,), (1,)), ((), ())), preferred_element_type=jnp.float32
+        )
+        scores = [
+            dots[:, j * BLOCK : (j + 1) * BLOCK] + jnp.minimum(live - 1 - j, 0).astype(jnp.float32) * 1e30
+            for j in range(listed)
+        ]
+        top = jnp.max(functools.reduce(jnp.maximum, scores), axis=1, keepdims=True)
+        weights = [jnp.exp((s - top) * scale) for s in scores]
+        total = jnp.sum(functools.reduce(jnp.add, weights), axis=1, keepdims=True)
+        rounded = jnp.concatenate([w.astype(jnp.bfloat16) for w in weights], axis=1)
+        value_part = jnp.concatenate([values[b] for b in blocks], axis=0)
+        mixed = jnp.dot(rounded, value_part, preferred_element_type=jnp.float32)
+        return (mixed / total).astype(jnp.bfloat16)
+
+    results = lax.map(one_head, (query_heads, key_heads, value_heads, keep))
+    joined = results.transpose(1, 0, 2).reshape(local_rows, heads_here * HEAD_DIM)
+    return lax.all_to_all(joined, "panel", split_axis=0, concat_axis=1, tiled=True)
+
+
+def spread_kernel(
+    n, panels, heads, trio,
+    lists, counts, q, k, v, out,
+    qf, kf, vf, qs, ks, vs, of, os,
+    fsend, frecv, qsend, qrecv, csend, crecv, wsend, osend, orecv,
+):
+    me = lax.axis_index("seq")
+    pan = lax.axis_index("panel")
+    chip, core = me // CORES, me % CORES
+    chips = n // CORES
+    sibling = chip * CORES + 1 - core
+    held = q.shape[0]
+    listed = lists.shape[1]
+    tiles = n * panels
+    scale = HEAD_DIM ** (-0.5)
+    flat = me * panels + pan
+
+    def columns(head):
+        return pl.ds(pl.multiple_of(head * HEAD_DIM, HEAD_DIM), HEAD_DIM)
+
+    def span(at, size):
+        return pl.ds(pl.multiple_of(at * size, size), size)
+
+    def whole_head(device):
+        return (device // CORES) * trio + device % CORES
+
+    def shared_head(device):
+        return (device // CORES) * trio + CORES
+
+    def full_copy(kind, step, device):
+        src, dst = ((k, kf), (q, qf), (v, vf))[kind]
+        return pltpu.make_async_remote_copy(
+            src_ref=src.at[:, :, columns(whole_head(device))],
+            dst_ref=dst.at[span(me, held)],
+            send_sem=fsend.at[kind, step],
+            recv_sem=frecv.at[kind, me],
+            device_id={"seq": device},
+            device_id_type=MESH,
+        )
+
+    def query_copy(step, device):
+        return pltpu.make_async_remote_copy(
+            src_ref=q.at[device % CORES, :, columns(shared_head(device))],
+            dst_ref=qs.at[me],
+            send_sem=qsend.at[step],
+            recv_sem=qrecv.at[me],
+            device_id={"seq": device},
+            device_id_type=MESH,
+        )
+
+    def shared_copy(kind, step, device):
+        src, dst = ((k, ks), (v, vs))[kind]
+        return pltpu.make_async_remote_copy(
+            src_ref=src.at[:, :, columns(shared_head(device))],
+            dst_ref=dst.at[span(me, held)],
+            send_sem=csend.at[kind, step],
+            recv_sem=crecv.at[kind, me],
+            device_id={"seq": device},
+            device_id_type=MESH,
+        )
+
+    def forward_copy(kind, step, origin):
+        buf = (ks, vs)[kind]
+        return pltpu.make_async_remote_copy(
+            src_ref=buf.at[span(origin, held)],
+            dst_ref=buf.at[span(origin, held)],
+            send_sem=wsend.at[kind, step],
+            recv_sem=crecv.at[kind, origin],
+            device_id={"seq": sibling},
+            device_id_type=MESH,
+        )
+
+    def result_copy(buf, index, slot, head, tile):
+        return pltpu.make_async_remote_copy(
+            src_ref=buf.at[index],
+            dst_ref=out.at[:, columns(pan * heads + head)],
+            send_sem=osend.at[slot],
+            recv_sem=orecv.at[pan * heads + head],
+            device_id={"seq": tile // panels, "panel": tile % panels},
+            device_id_type=MESH,
+        )
+
+    barrier = pltpu.get_barrier_semaphore()
+
+    def greet(step, carry):
+        other = (flat + step) % (n * panels)
+        pl.semaphore_signal(
+            barrier, inc=1,
+            device_id={"seq": other // panels, "panel": other % panels},
+            device_id_type=MESH,
+        )
+        return carry
+
+    lax.fori_loop(1, n * panels, greet, 0)
+
+    own = [
+        pltpu.make_async_copy(src.at[:, :, columns(whole_head(me))], dst.at[span(me, held)], frecv.at[kind, me])
+        for kind, (src, dst) in enumerate(((k, kf), (q, qf), (v, vf)))
+    ]
+    own.append(
+        pltpu.make_async_copy(
+            q.at[core, :, columns(shared_head(me))], qs.at[me], qrecv.at[me]
+        )
+    )
+    own += [
+        pltpu.make_async_copy(src.at[:, :, columns(shared_head(me))], dst.at[span(me, held)], crecv.at[kind, me])
+        for kind, (src, dst) in enumerate(((k, ks), (v, vs)))
+    ]
+    for copy in own:
+        copy.start()
+
+    pl.semaphore_wait(barrier, n * panels - 1)
+
+    def send_full(step, carry):
+        device = (me + step) % n
+        for kind in range(3):
+            full_copy(kind, step, device).start()
+        return carry
+
+    lax.fori_loop(1, n, send_full, 0)
+
+    def sent_full(step):
+        for kind in range(3):
+            full_copy(kind, step, (me + step) % n).wait_send()
         query_copy(step, (me + step) % n).start()
-        return carry
-
-    lax.fori_loop(1, n, send_query, 0)
+
+    def send_shared(step, carry):
+        sent_full(CORES * step - 1)
+        sent_full(CORES * step)
+        device = ((chip + step) % chips) * CORES + core
+        for kind in range(2):
+            shared_copy(kind, step, device).start()
+        return carry
+
+    lax.fori_loop(1, chips, send_shared, 0)
+    sent_full(n - 1)
+    for kind in range(2):
+        shared_copy(kind, 0, sibling).start()
 
     def attend(query, head, tile, keys, values):
-        blocks = [lists[head, tile, j] for j in range(listed)]
+        blocks = [lists[head, j, tile] for j in range(listed)]
         live = counts[head, tile]
         scores = []
         for j in range(listed):
@@ -291,8 +456,6 @@
 
     def finish_sends(step, carry):
         device = (me + step) % n
-        for kind in range(3):
-            full_copy(kind, step, device).wait_send()
         query_copy(step, device).wait_send()
         return carry
 
@@ -361,10 +524,10 @@
             dma((tiles + n,)), dma((heads * panels,)),
         ],
         compiler_params=pltpu.CompilerParams(
-            collective_id=0, has_side_effects=True, vmem_limit_bytes=48 * 1024 * 1024
+            collective_id=0, has_side_effects=True, vmem_limit_bytes=62 * 1024 * 1024
         ),
         name="spread_heads",
-    )(block_lists, block_counts, *(x.reshape(-1, BLOCK, width) for x in (queries, key_rows, value_rows)))
+    )(block_lists.transpose(0, 2, 1), block_counts, *(x.reshape(-1, BLOCK, width) for x in (queries, key_rows, value_rows)))
 
 
 def solution(mesh):

time: 84.3 us -> 81.2 us (0.963)
  local copies, waits for them, and re-layouts: 5.17 us -> 2.06 us
    unnamed x10 -> x1, local copies, waits for them, and re-layouts: 5.17 us -> 2.06 us
where the time goes in v2:
time: 81.2 us; the launch traced here: 80.9 us
  Pallas kernels  78.8 us (97%)
  local copies, waits for them, and re-layouts  2.06 us (3%)
    pallas_call x1, Pallas kernels, spread(): pl.pallas_call(functools.partial(spread_kernel, n, panels, heads, trio),...  78.8 us
    unnamed x1, local copies, waits for them, and re-layouts  2.06 us

profile of v2, /device:TPU:0, one launch (start us, length us, event | category | flops | bytes accessed | tf_op | source)
XLA Modules:
  0.0 80.9 jit_solution(10614048135916877612)
XLA Ops:
  0.0 78.8 %spread_heads.1 = bf16[128,3072]{1,0:T(8,128)(2,1)} custom-call(s32[12,8,16]{2,1,0:T(8,128)} %bitcast.7, s32[12,16]{1,0:T(8,128)} %counts.1, bf16[2,128,1536]{2,1,0:T(8,128)(2,1)} %bitcast.4, bf16[2,128,1536]{2,1,0:T(8,128)(2,1)} %bitcast.5, bf16[2,128,1536]{2,1,0:T(8,128)(2,1)} %bitcast.6), custom_call_target="tpu_custom_call" | custom-call | tf_op jit(solution)/shard_map/spread_heads/pallas_call | solution.py:511
  78.8 2.1 %copy.7 = bf16[128,3072]{1,0:T(8,128)(2,1)} copy(bf16[128,3072]{1,0:T(8,128)(2,1)} %spread_heads.1) | data formatting | bytes 1572864

commit v3 on v1

--- a/solution.py
+++ b/solution.py
@@ -66,10 +66,27 @@
     chips = n // CORES
     sibling = chip * CORES + 1 - core
     held = q.shape[0]
-    listed = lists.shape[2]
+    listed = lists.shape[1]
     tiles = n * panels
     scale = HEAD_DIM ** (-0.5)
     flat = me * panels + pan
+
+    half, side = n // 2, me // (n // 2)
+
+    def peer(step):
+        far = (1 - side) * half + (me + step) % half
+        near = side * half + (me + step + 1) % half
+        return jnp.where(step < half, far, near)
+
+    def peer_or_me(step):
+        return jnp.where(step == n - 1, me, peer(step))
+
+    def chip_peer(step):
+        many = chips // 2
+        where = chip // many
+        far = (1 - where) * many + (chip + step) % many
+        near = where * many + (chip + step + 1) % many
+        return jnp.where(step < many, far, near) * CORES + core
 
     def columns(head):
         return pl.ds(pl.multiple_of(head * HEAD_DIM, HEAD_DIM), HEAD_DIM)
@@ -168,49 +185,44 @@
     pl.semaphore_wait(barrier, n * panels - 1)
 
     def send_full(step, carry):
-        device = (me + step) % n
         for kind in range(3):
-            full_copy(kind, step, device).start()
-        return carry
-
-    lax.fori_loop(1, n, send_full, 0)
+            full_copy(kind, step, peer(step)).start()
+        return carry
+
+    lax.fori_loop(0, n - 1, send_full, 0)
 
     def send_shared(step, carry):
-        device = ((chip + step) % chips) * CORES + core
         for kind in range(2):
-            shared_copy(kind, step, device).start()
-        return carry
-
-    lax.fori_loop(1, chips, send_shared, 0)
+            shared_copy(kind, step, chip_peer(step)).start()
+        return carry
+
+    lax.fori_loop(0, chips - 1, send_shared, 0)
     for kind in range(2):
-        shared_copy(kind, 0, sibling).start()
+        shared_copy(kind, chips - 1, sibling).start()
 
     def send_query(step, carry):
-        query_copy(step, (me + step) % n).start()
-        return carry
-
-    lax.fori_loop(1, n, send_query, 0)
+        query_copy(step, peer(step)).start()
+        return carry
+
+    lax.fori_loop(0, n - 1, send_query, 0)
 
     def attend(query, head, tile, keys, values):
-        blocks = [lists[head, tile, j] for j in range(listed)]
+        blocks = [lists[head, j, tile] for j in range(listed)]
         live = counts[head, tile]
-        scores = []
-        for j in range(listed):
-            dots = lax.dot_general(
-                query, keys[blocks[j]], (((1,), (1,)), ((), ())), preferred_element_type=jnp.float32
-            )
-            scores.append(dots + jnp.minimum(live - 1 - j, 0).astype(jnp.float32) * 1e30)
-        top = functools.reduce(jnp.maximum, scores)
-        top = jnp.max(top, axis=1, keepdims=True)
+        key_part = jnp.concatenate([keys[b] for b in blocks], axis=0)
+        dots = lax.dot_general(
+            query, key_part, (((1,), (1,)), ((), ())), preferred_element_type=jnp.float32
+        )
+        scores = [
+            dots[:, j * BLOCK : (j + 1) * BLOCK] + jnp.minimum(live - 1 - j, 0).astype(jnp.float32) * 1e30
+            for j in range(listed)
+        ]
+        top = jnp.max(functools.reduce(jnp.maximum, scores), axis=1, keepdims=True)
         weights = [jnp.exp((s - top) * scale) for s in scores]
         total = jnp.sum(functools.reduce(jnp.add, weights), axis=1, keepdims=True)
-        mixed = functools.reduce(
-            jnp.add,
-            [
-                jnp.dot(w.astype(jnp.bfloat16), values[blocks[j]], preferred_element_type=jnp.float32)
-                for j, w in enumerate(weights)
-            ],
-        )
+        rounded = jnp.concatenate([w.astype(jnp.bfloat16) for w in weights], axis=1)
+        value_part = jnp.concatenate([values[b] for b in blocks], axis=0)
+        mixed = jnp.dot(rounded, value_part, preferred_element_type=jnp.float32)
         return (mixed / total).astype(jnp.bfloat16)
 
     def ship(buf, index, slot, head, tile):
@@ -236,7 +248,7 @@
     lax.fori_loop(0, n, wait_full, 0)
 
     def full_pair(step, carry):
-        device = (me + step) % n
+        device = peer_or_me(step)
         mine = whole_head(me)
         for place in range(panels):
             tile = device * panels + place
@@ -244,7 +256,7 @@
             ship(of, tile, tile, mine, tile)
         return carry
 
-    lax.fori_loop(1, n + 1, full_pair, 0)
+    lax.fori_loop(0, n, full_pair, 0)
 
     def wait_shared(kind, origin):
         ref, dst = ((k, ks), (v, vs))[kind]
@@ -253,13 +265,13 @@
         ).wait()
 
     def forward(step, carry):
-        origin = ((chip + step) % chips) * CORES + core
+        origin = chip_peer(chips - 2 - step)
         for kind in range(2):
             wait_shared(kind, origin)
-            forward_copy(kind, step, origin).start()
-        return carry
-
-    lax.fori_loop(1, chips, forward, 0)
+            forward_copy(kind, chips - 2 - step, origin).start()
+        return carry
+
+    lax.fori_loop(0, chips - 1, forward, 0)
     for kind in range(2):
         wait_shared(kind, me)
 
@@ -281,7 +293,7 @@
     def half_pair(step, carry):
         mine = shared_head(me)
         for place in range(2):
-            device = (me + 1 + step * 2 + place) % n
+            device = peer_or_me(step * 2 + place)
             tile = device * panels + core
             os[device] = attend(qs[device], mine, tile, ks, vs)
             ship(os, device, tiles + device, mine, tile)
@@ -290,24 +302,22 @@
     lax.fori_loop(0, n // 2, half_pair, 0)
 
     def finish_sends(step, carry):
-        device = (me + step) % n
         for kind in range(3):
-            full_copy(kind, step, device).wait_send()
-        query_copy(step, device).wait_send()
-        return carry
-
-    lax.fori_loop(1, n, finish_sends, 0)
+            full_copy(kind, step, peer(step)).wait_send()
+        query_copy(step, peer(step)).wait_send()
+        return carry
+
+    lax.fori_loop(0, n - 1, finish_sends, 0)
 
     def finish_shared(step, carry):
-        device = ((chip + step) % chips) * CORES + core
         for kind in range(2):
-            shared_copy(kind, step, device).wait_send()
-            forward_copy(kind, step, device).wait_send()
-        return carry
-
-    lax.fori_loop(1, chips, finish_shared, 0)
+            shared_copy(kind, step, chip_peer(step)).wait_send()
+            forward_copy(kind, step, chip_peer(step)).wait_send()
+        return carry
+
+    lax.fori_loop(0, chips - 1, finish_shared, 0)
     for kind in range(2):
-        shared_copy(kind, 0, sibling).wait_send()
+        shared_copy(kind, chips - 1, sibling).wait_send()
 
     def finish_full_results(step, carry):
         tile = (flat + step) % tiles
@@ -349,7 +359,7 @@
         functools.partial(spread_kernel, n, panels, heads, trio),
         out_shape=jax.ShapeDtypeStruct((BLOCK, width * panels), kind),
         in_specs=[smem, smem, anywhere, anywhere, anywhere],
-        out_specs=anywhere,
+        out_specs=pl.BlockSpec(memory_space=pltpu.VMEM),
         scratch_shapes=[
             whole, whole, whole,
             pltpu.VMEM((n, BLOCK, HEAD_DIM), kind), whole, whole,
@@ -361,10 +371,10 @@
             dma((tiles + n,)), dma((heads * panels,)),
         ],
         compiler_params=pltpu.CompilerParams(
-            collective_id=0, has_side_effects=True, vmem_limit_bytes=48 * 1024 * 1024
+            collective_id=0, has_side_effects=True, vmem_limit_bytes=62 * 1024 * 1024
         ),
         name="spread_heads",
-    )(block_lists, block_counts, *(x.reshape(-1, BLOCK, width) for x in (queries, key_rows, value_rows)))
+    )(block_lists.transpose(0, 2, 1), block_counts, *(x.reshape(-1, BLOCK, width) for x in (queries, key_rows, value_rows)))
 
 
 def solution(mesh):
@@ -374,7 +384,7 @@
         rows, width = queries.shape
         heads = width // HEAD_DIM
         fits = (
-            n % CORES == 0
+            n % (2 * CORES) == 0
             and panels == CORES
             and rows == panels * BLOCK
             and CORES * heads == (CORES + 1) * n

time: 84.3 us -> 79.8 us (0.947)
  local copies, waits for them, and re-layouts: 5.17 us -> 2.06 us
  Pallas kernels: 78.6 us -> 77 us
    unnamed x10 -> x1, local copies, waits for them, and re-layouts: 5.17 us -> 2.06 us
    pallas_call x1, Pallas kernels: 78.6 us -> 77 us  [spread(): pl.pallas_call(functools.partial(spread_kernel, n, panels, heads, trio),...]
where the time goes in v3:
time: 79.8 us; the launch traced here: 79 us
  Pallas kernels  77 us (96%)
  local copies, waits for them, and re-layouts  2.06 us (3%)
    pallas_call x1, Pallas kernels, spread(): pl.pallas_call(functools.partial(spread_kernel, n, panels, heads, trio),...  77 us
    unnamed x1, local copies, waits for them, and re-layouts  2.06 us

profile of v3, /device:TPU:0, one launch (start us, length us, event | category | flops | bytes accessed | tf_op | source)
XLA Modules:
  0.0 79.0 jit_solution(14897069822450097038)
XLA Ops:
  0.0 77.0 %spread_heads.1 = bf16[128,3072]{1,0:T(8,128)(2,1)} custom-call(s32[12,8,16]{2,1,0:T(8,128)} %bitcast.7, s32[12,16]{1,0:T(8,128)} %counts.1, bf16[2,128,1536]{2,1,0:T(8,128)(2,1)} %bitcast.4, bf16[2,128,1536]{2,1,0:T(8,128)(2,1)} %bitcast.5, bf16[2,128,1536]{2,1,0:T(8,128)(2,1)} %bitcast.6), custom_call_target="tpu_custom_call" | custom-call | tf_op jit(solution)/shard_map/spread_heads/pallas_call | solution.py:358
  77.0 2.1 %copy.7 = bf16[128,3072]{1,0:T(8,128)(2,1)} copy(bf16[128,3072]{1,0:T(8,128)(2,1)} %spread_heads.1) | data formatting | bytes 1572864

commit v4 on v3

--- a/solution.py
+++ b/solution.py
@@ -56,9 +56,9 @@
 
 def spread_kernel(
     n, panels, heads, trio,
-    lists, counts, q, k, v, out,
+    lists, counts, q, k, v, out, sq, sk, sv,
     qf, kf, vf, qs, ks, vs, of, os,
-    fsend, frecv, qsend, qrecv, csend, crecv, wsend, osend, orecv,
+    staged, fsend, frecv, qsend, qrecv, csend, crecv, wsend, osend, orecv,
 ):
     me = lax.axis_index("seq")
     pan = lax.axis_index("panel")
@@ -101,9 +101,9 @@
         return (device // CORES) * trio + CORES
 
     def full_copy(kind, step, device):
-        src, dst = ((k, kf), (q, qf), (v, vf))[kind]
+        src, dst = ((sk, kf), (sq, qf), (sv, vf))[kind]
         return pltpu.make_async_remote_copy(
-            src_ref=src.at[:, :, columns(whole_head(device))],
+            src_ref=src.at[whole_head(device)],
             dst_ref=dst.at[span(me, held)],
             send_sem=fsend.at[kind, step],
             recv_sem=frecv.at[kind, me],
@@ -113,7 +113,7 @@
 
     def query_copy(step, device):
         return pltpu.make_async_remote_copy(
-            src_ref=q.at[device % CORES, :, columns(shared_head(device))],
+            src_ref=sq.at[shared_head(device), device % CORES],
             dst_ref=qs.at[me],
             send_sem=qsend.at[step],
             recv_sem=qrecv.at[me],
@@ -122,9 +122,9 @@
         )
 
     def shared_copy(kind, step, device):
-        src, dst = ((k, ks), (v, vs))[kind]
+        src, dst = ((sk, ks), (sv, vs))[kind]
         return pltpu.make_async_remote_copy(
-            src_ref=src.at[:, :, columns(shared_head(device))],
+            src_ref=src.at[shared_head(device)],
             dst_ref=dst.at[span(me, held)],
             send_sem=csend.at[kind, step],
             recv_sem=crecv.at[kind, me],
@@ -179,10 +179,25 @@
         pltpu.make_async_copy(src.at[:, :, columns(shared_head(me))], dst.at[span(me, held)], crecv.at[kind, me])
         for kind, (src, dst) in enumerate(((k, ks), (v, vs)))
     ]
+    def stage(kind, head):
+        src, dst = ((k, sk), (q, sq), (v, sv))[kind]
+        return pltpu.make_async_copy(src.at[:, :, columns(head)], dst.at[head], staged.at[kind, head])
+
+    def start_stage(head, carry):
+        for kind in range(3):
+            stage(kind, head).start()
+        return carry
+
+    def wait_stage(head, carry):
+        for kind in range(3):
+            stage(kind, head).wait()
+        return carry
+
+    lax.fori_loop(0, heads, start_stage, 0)
+    pl.semaphore_wait(barrier, n * panels - 1)
+    lax.fori_loop(0, heads, wait_stage, 0)
     for copy in own:
         copy.start()
-
-    pl.semaphore_wait(barrier, n * panels - 1)
 
     def send_full(step, carry):
         for kind in range(3):
@@ -355,17 +370,19 @@
     chips = n // CORES
     smem = pl.BlockSpec(memory_space=pltpu.SMEM)
     anywhere = pl.BlockSpec(memory_space=pl.ANY)
+    piled = pltpu.VMEM((heads, rows // BLOCK, BLOCK, HEAD_DIM), kind)
     return pl.pallas_call(
         functools.partial(spread_kernel, n, panels, heads, trio),
         out_shape=jax.ShapeDtypeStruct((BLOCK, width * panels), kind),
         in_specs=[smem, smem, anywhere, anywhere, anywhere],
-        out_specs=pl.BlockSpec(memory_space=pltpu.VMEM),
+        out_specs=anywhere,
         scratch_shapes=[
+            piled, piled, piled,
             whole, whole, whole,
             pltpu.VMEM((n, BLOCK, HEAD_DIM), kind), whole, whole,
             pltpu.VMEM((tiles, BLOCK, HEAD_DIM), kind),
             pltpu.VMEM((n, BLOCK, HEAD_DIM), kind),
-            dma((3, n)), dma((3, n)),
+            dma((3, heads)), dma((3, n)), dma((3, n)),
             dma((n,)), dma((n,)),
             dma((2, chips)), dma((2, n)), dma((2, chips)),
             dma((tiles + n,)), dma((heads * panels,)),

time: 79.8 us -> 79.7 us (level)
  no operation moved by 1% of the time
where the time goes in v4:
time: 79.7 us; the launch traced here: 79.3 us
  Pallas kernels  77.2 us (97%)
  local copies, waits for them, and re-layouts  2.06 us (3%)
    pallas_call x1, Pallas kernels, spread(): pl.pallas_call(functools.partial(spread_kernel, n, panels, heads, trio),...  77.2 us
    unnamed x1, local copies, waits for them, and re-layouts  2.06 us

profile of v4, /device:TPU:0, one launch (start us, length us, event | category | flops | bytes accessed | tf_op | source)
XLA Modules:
  0.0 79.3 jit_solution(1723508171867911606)
XLA Ops:
  0.0 77.2 %spread_heads.1 = bf16[128,3072]{1,0:T(8,128)(2,1)} custom-call(s32[12,8,16]{2,1,0:T(8,128)} %bitcast.7, s32[12,16]{1,0:T(8,128)} %counts.1, bf16[2,128,1536]{2,1,0:T(8,128)(2,1)} %bitcast.4, bf16[2,128,1536]{2,1,0:T(8,128)(2,1)} %bitcast.5, bf16[2,128,1536]{2,1,0:T(8,128)(2,1)} %bitcast.6), custom_call_target="tpu_custom_call" | custom-call | tf_op jit(solution)/shard_map/spread_heads/pallas_call | solution.py:374
  77.2 2.1 %copy.7 = bf16[128,3072]{1,0:T(8,128)(2,1)} copy(bf16[128,3072]{1,0:T(8,128)(2,1)} %spread_heads.1) | data formatting | bytes 1572864
